TPU v7x, 32 devices: a whole 2x2x4 slice. The times are simulated.
32 devices in a mesh: fsdp: 16 (over z, y, x), dp: 2 (over core).
Axes of the slice: x: 2, y: 2, z: 4, core: 2. Of those that a mesh axis runs over, the one named last changes fastest.
Arguments:
- tokens: bfloat16 [4096, 8192], P(('fsdp', 'dp')), may hold values from -6 to 6
- token_adapter_index: int32 [4096, 1], P(('fsdp', 'dp')), may hold values from 0 to 15; in each aligned block of 128 rows (0 to 127, 128 to 255, ...) at most 12 rows name the same one
- adapter_storage_index: int32 [16], replicated, may hold values from 0 to 15, each once
- frozen_value_weight: bfloat16 [8192, 512], P(('fsdp', 'dp')), may hold values from -0.0625 to 0.0625
- frozen_value_bias: bfloat16 [512], replicated, may hold values from -3 to 3
- adapter_down_weight: bfloat16 [16, 8192, 64], P('fsdp'), may hold values from -0.0625 to 0.0625
- adapter_up_weight: bfloat16 [16, 64, 512], P('fsdp'), may hold values from -0.75 to 0.75
- cotangent: bfloat16 [4096, 512], P(('fsdp', 'dp')), may hold values from -0.1875 to 0.1875
Outputs:
- values: bfloat16 [4096, 512], P(('fsdp', 'dp'))
- grad_down: float32 [16, 8192, 64], P('fsdp', 'dp')
- grad_up: float32 [16, 64, 512], P('fsdp', None, 'dp')
Inputs may be any that keep to these rules, and one draw needn't show every extreme that they name: `token_adapter_index`: within the 128 rows of one device no adapter is named by more than 12 rows. `adapter_storage_index`: each storage index appears once.
All inputs are finite; a program needn't handle non-finite values.
Results may differ from a plain program's by a relative error of at most 0.0048.
Values may be sent and summed in bfloat16 or wider, within the bound.
A program may use at most 64 MiB of HBM per device.

v0:
```python
import jax
import jax.numpy as jnp
from jax import lax
from jax.sharding import PartitionSpec as P


def body(
    tokens,
    token_adapter_index,
    adapter_storage_index,
    frozen_value_weight,
    frozen_value_bias,
    adapter_down_weight,
    adapter_up_weight,
    cotangent,
):
    token_count, model_width = tokens.shape
    value_width = frozen_value_weight.shape[1]
    fsdp_size = lax.axis_size("fsdp")
    slots_total = adapter_storage_index.shape[0]
    capacity = max(2, (3 * token_count + 2 * fsdp_size - 1) // (2 * fsdp_size))
    base_value = jnp.dot(
        tokens,
        lax.all_gather(frozen_value_weight, ("fsdp", "dp"), axis=0, tiled=True),
        preferred_element_type=jnp.float32,
    )
    base_value = base_value + frozen_value_bias.astype(jnp.float32)
    owner_index = jnp.take(adapter_storage_index, token_adapter_index[:, 0])
    onehot = (owner_index[:, None] == jnp.arange(slots_total)[None, :]).astype(jnp.int32)
    place_in_slot = jnp.sum((jnp.cumsum(onehot, 0) - onehot) * onehot, 1)
    target_row = owner_index * capacity + place_in_slot
    dispatch = (jnp.arange(slots_total * capacity)[:, None] == target_row[None, :]).astype(
        jnp.bfloat16
    )
    sent_rows = jnp.dot(dispatch, tokens, preferred_element_type=jnp.float32).astype(jnp.bfloat16)
    sent_rows = sent_rows.reshape(slots_total, capacity, model_width)
    sent_cot = jnp.dot(dispatch, cotangent, preferred_element_type=jnp.float32).astype(jnp.bfloat16)
    sent_cot = sent_cot.reshape(slots_total, capacity, value_width)
    arrived = lax.all_to_all(sent_rows, "fsdp", split_axis=0, concat_axis=0, tiled=True)
    arrived_rows = arrived.reshape(-1, model_width)
    down_projection = adapter_down_weight[0]
    up_projection = adapter_up_weight[0]
    rank_activation = jnp.dot(
        arrived_rows, down_projection, preferred_element_type=jnp.float32
    ).astype(jnp.bfloat16)
    adapter_delta = jnp.dot(
        rank_activation, up_projection, preferred_element_type=jnp.float32
    ).astype(jnp.bfloat16)
    returned = lax.all_to_all(
        adapter_delta.reshape(fsdp_size, capacity, value_width),
        "fsdp",
        split_axis=0,
        concat_axis=0,
        tiled=True,
    )
    returned = returned.reshape(-1, value_width)
    placed = jnp.einsum("st,sk->tk", dispatch, returned, preferred_element_type=jnp.float32)
    values = (base_value + placed).astype(jnp.bfloat16)
    arrived_cot = lax.all_to_all(sent_cot, "fsdp", split_axis=0, concat_axis=0, tiled=True)
    cotangent_rows = arrived_cot.reshape(-1, value_width)
    rank_cotangent = lax.dot_general(
        cotangent_rows, up_projection, (((1,), (1,)), ((), ())), preferred_element_type=jnp.float32
    ).astype(jnp.bfloat16)
    grad_down = lax.dot_general(
        arrived_rows, rank_cotangent, (((0,), (0,)), ((), ())), preferred_element_type=jnp.float32
    )
    grad_up = lax.dot_general(
        rank_activation,
        cotangent_rows,
        (((0,), (0,)), ((), ())),
        preferred_element_type=jnp.float32,
    )
    summed_down, summed_up = (
        lax.psum_scatter(grad_down, "dp", scatter_dimension=0, tiled=True),
        lax.psum_scatter(grad_up, "dp", scatter_dimension=1, tiled=True),
    )
    return (values, summed_down[None], summed_up[None])


def solution(mesh):
    return jax.shard_map(
        body,
        mesh=mesh,
        in_specs=(
            P(("fsdp", "dp"), None),
            P(("fsdp", "dp"), None),
            P(),
            P(("fsdp", "dp"), None),
            P(),
            P("fsdp", None, None),
            P("fsdp", None, None),
            P(("fsdp", "dp"), None),
        ),
        out_specs=(P(("fsdp", "dp"), None), P("fsdp", "dp", None), P("fsdp", None, "dp")),
        check_vma=False,
    )
```

profile of v0, /device:TPU:0, one launch (start us, length us, event | category | flops | bytes accessed | tf_op | source)
XLA Modules:
  0.0 211.8 jit_solution(7064073073282243629)
XLA Ops:
  8.1 0.7 all-gather.2.cloned.1.call-update
  8.7 2.0 fusion.14
  10.7 10.6 %fusion.13 = (s32[128]{0:T(128)S(1)}, s32[128]{0:T(128)S(1)}) fusion(s32[128,1]{0,1:T(1,128)} %param.9, s32[]{:T(128)} %bitcast.25, s32[]{:T(128)} %bitcast.24, s32[]{:T(128)} %bitcast.23, s32[]{:T(128)} %bitcast.22, s32[]{:T(128)} %bitcast.21, s32[]{:T(128)} %bitcast.20, s32[]{:T(128)} %bitcast.19, s32[]{:T(128)} %bitcast.18, s32[]{:T(128)} %bitcast.16, ...), kind=kLoop, calls=%fused_computation.41 | loop fusion | flops 4736 | bytes 1600 | tf_op jit(solution)/shard_map/eq | solution.py:29
  21.4 0.2 reduce_window_sum.11
  21.6 0.2 select_reduce_fusion
  21.8 0.7 fusion.12
  22.4 1.1 convolution_convert_fusion.2
  23.5 0.8 reshape.45
  24.3 8.3 %all-to-all-start.2 = ((bf16[16,12,512]{2,1,0:T(8,128)(2,1)}), bf16[16,12,512]{2,1,0:T(8,128)(2,1)S(1)}, u32[]{:S(2)}, u32[]{:S(2)}) async-start(bf16[16,12,512]{2,1,0:T(8,128)(2,1)} %reshape.45), calls=%async_computation.2 | async-start | bytes 524288 | tf_op jit(solution)/shard_map/all_to_all | solution.py:59
  32.6 2.7 %convolution_convert_fusion = bf16[192,8192]{1,0:T(8,128)(2,1)} fusion(bf16[128,8192]{1,0:T(8,128)(2,1)S(1)} %copy-done, s32[128]{0:T(128)S(1)} %fusion.12), kind=kOutput, calls=%fused_computation | convolution fusion | flops 404250624 | bytes 5243392 | tf_op jit(solution)/shard_map/dot_general | solution.py:35
  35.3 4.7 %reshape.41 = bf16[16,12,8192]{2,1,0:T(8,128)(2,1)} reshape(bf16[192,8192]{1,0:T(8,128)(2,1)} %convolution_convert_fusion) | data formatting | bytes 6291456 | tf_op jit(solution)/shard_map/reshape | solution.py:36
  40.0 2.8 %all-to-all-done.2 = bf16[16,12,512]{2,1,0:T(8,128)(2,1)S(1)} async-done(((bf16[16,12,512]{2,1,0:T(8,128)(2,1)}), bf16[16,12,512]{2,1,0:T(8,128)(2,1)S(1)}, u32[]{:S(2)}, u32[]{:S(2)}) %all-to-all-start.2) | async-done | bytes 196640 | tf_op jit(solution)/shard_map/all_to_all | solution.py:59
  42.9 4.6 %all-to-all-start = ((bf16[16,12,8192]{2,1,0:T(8,128)(2,1)}), bf16[16,12,8192]{2,1,0:T(8,128)(2,1)}, u32[]{:S(2)}, u32[]{:S(2)}) async-start(bf16[16,12,8192]{2,1,0:T(8,128)(2,1)} %reshape.41), calls=%async_computation | async-start | bytes 8388608 | tf_op jit(solution)/shard_map/all_to_all | solution.py:39
  47.6 107.3 %all-to-all-done = bf16[16,12,8192]{2,1,0:T(8,128)(2,1)} async-done(((bf16[16,12,8192]{2,1,0:T(8,128)(2,1)}), bf16[16,12,8192]{2,1,0:T(8,128)(2,1)}, u32[]{:S(2)}, u32[]{:S(2)}) %all-to-all-start) | async-done | bytes 3145760 | tf_op jit(solution)/shard_map/all_to_all | solution.py:39
  154.9 4.8 %reshape.42 = bf16[192,8192]{1,0:T(8,128)(2,1)} reshape(bf16[16,12,8192]{2,1,0:T(8,128)(2,1)} %all-to-all-done) | data formatting | bytes 6291456 | tf_op jit(solution)/shard_map/reshape | solution.py:40
  159.6 3.0 %convolution_convert_fusion.4 = bf16[192,64]{0,1:T(8,128)(2,1)S(1)} fusion(bf16[192,8192]{1,0:T(8,128)(2,1)} %reshape.42, bf16[1,8192,64]{1,2,0:T(8,128)(2,1)S(1)} %copy-done.1), kind=kOutput, calls=%fused_computation.7 | convolution fusion | flops 201338880 | bytes 4218880 | tf_op jit(solution)/shard_map/dot_general | solution.py:43
  162.7 0.8 fusion.15
  163.6 4.2 %fusion.1 = f32[8192,64]{0,1:T(8,128)} fusion(bf16[192,8192]{1,0:T(8,128)(2,1)} %reshape.42, bf16[192,512]{1,0:T(8,128)(2,1)S(1)} %reshape.46, bf16[1,64,512]{2,1,0:T(8,128)(2,1)S(1)} %copy-done.2), kind=kOutput, calls=%fused_computation.8 | convolution fusion | flops 213921792 | bytes 5505024 | tf_op jit(solution)/shard_map/dot_general | solution.py:64
  167.9 0.2 convolution_convert_fusion.1
  168.1 0.8 reshape.43
  168.9 20.3 %all-to-all-start.1 = ((bf16[16,12,512]{2,1,0:T(8,128)(2,1)}), bf16[16,12,512]{2,1,0:T(8,128)(2,1)S(1)}, u32[]{:S(2)}, u32[]{:S(2)}) async-start(bf16[16,12,512]{2,1,0:T(8,128)(2,1)} %reshape.43), calls=%async_computation.1 | async-start | bytes 524288 | tf_op jit(solution)/shard_map/all_to_all | solution.py:49
  189.2 9.6 %all-to-all-done.1 = bf16[16,12,512]{2,1,0:T(8,128)(2,1)S(1)} async-done(((bf16[16,12,512]{2,1,0:T(8,128)(2,1)}), bf16[16,12,512]{2,1,0:T(8,128)(2,1)S(1)}, u32[]{:S(2)}, u32[]{:S(2)}) %all-to-all-start.1) | async-done | bytes 196640 | tf_op jit(solution)/shard_map/all_to_all | solution.py:49
  198.8 4.7 %convolution_add_fusion.1 = f32[128,512]{1,0:T(8,128)S(1)} fusion(bf16[128,8192]{1,0:T(8,128)(2,1)S(1)} %copy-done, bf16[8192,512]{1,0:T(8,128)(2,1)} %all-gather.2.cloned.1.call-done, f32[512]{0:T(512)S(1)} %convert_element_type.25), kind=kOutput, calls=%fused_computation.4 | convolution fusion | flops 1073807360 | bytes 10749952 | tf_op jit(solution)/shard_map/dot_general | solution.py:22
  203.5 0.9 fusion
  (20 shorter events, 0.4 us)
Async XLA Ops:
  8.0 24.6 %copy-start = (bf16[128,8192]{1,0:T(8,128)(2,1)S(1)}, bf16[128,8192]{1,0:T(8,128)(2,1)}, u32[]{:S(2)}) copy-start(bf16[128,8192]{1,0:T(8,128)(2,1)} %param.8) | copy-start | bytes 6291460
  8.0 190.8 %all-gather.2.cloned.1.call-start = ((), (), s32[]{:S(2)}) async-start(), calls=%async_computation.5 | async-start | bytes 8650752 | tf_op jit(solution)/shard_map/all_gather | solution.py:24
  24.3 18.6 %all-to-all-start.2 = ((bf16[16,12,512]{2,1,0:T(8,128)(2,1)}), bf16[16,12,512]{2,1,0:T(8,128)(2,1)S(1)}, u32[]{:S(2)}, u32[]{:S(2)}) async-start(bf16[16,12,512]{2,1,0:T(8,128)(2,1)} %reshape.45), calls=%async_computation.2 | async-start | bytes 524288 | tf_op jit(solution)/shard_map/all_to_all | solution.py:59
  42.9 112.0 %all-to-all-start = ((bf16[16,12,8192]{2,1,0:T(8,128)(2,1)}), bf16[16,12,8192]{2,1,0:T(8,128)(2,1)}, u32[]{:S(2)}, u32[]{:S(2)}) async-start(bf16[16,12,8192]{2,1,0:T(8,128)(2,1)} %reshape.41), calls=%async_computation | async-start | bytes 8388608 | tf_op jit(solution)/shard_map/all_to_all | solution.py:39
  47.4 156.9 %reduce-scatter.5.cloned.1.call-start = ((), (), s32[]{:S(2)}) async-start(), calls=%async_computation.7 | async-start | bytes 196608 | tf_op jit(solution)/shard_map/reduce_scatter | solution.py:75
  47.5 112.1 %copy-start.1 = (bf16[1,8192,64]{1,2,0:T(8,128)(2,1)S(1)}, bf16[1,8192,64]{1,2,0:T(8,128)(2,1)}, u32[]{:S(2)}) copy-start(bf16[1,8192,64]{1,2,0:T(8,128)(2,1)} %param.13) | copy-start | bytes 3145732
  159.6 4.0 %copy-start.2 = (bf16[1,64,512]{2,1,0:T(8,128)(2,1)S(1)}, bf16[1,64,512]{2,1,0:T(8,128)(2,1)}, u32[]{:S(2)}) copy-start(bf16[1,64,512]{2,1,0:T(8,128)(2,1)} %param.14) | copy-start | bytes 196612
  163.5 25.6 %copy-start.3 = (bf16[512]{0:T(512)(128)(2,1)S(1)}, bf16[512]{0:T(512)(128)(2,1)}, u32[]{:S(2)}) copy-start(bf16[512]{0:T(512)(128)(2,1)} %param.12) | copy-start | bytes 3076
  163.5 40.8 %reduce-scatter.3.cloned.1.call-start = ((), (), s32[]{:S(2)}) async-start(), calls=%async_computation.6 | async-start | bytes 3145728 | tf_op jit(solution)/shard_map/reduce_scatter | solution.py:74
  168.9 29.9 %all-to-all-start.1 = ((bf16[16,12,512]{2,1,0:T(8,128)(2,1)}), bf16[16,12,512]{2,1,0:T(8,128)(2,1)S(1)}, u32[]{:S(2)}, u32[]{:S(2)}) async-start(bf16[16,12,512]{2,1,0:T(8,128)(2,1)} %reshape.43), calls=%async_computation.1 | async-start | bytes 524288 | tf_op jit(solution)/shard_map/all_to_all | solution.py:49
Sparse Core Ops, SparseCore 0:
  11.7 137.8 all-gather.1
Sparse Core Ops, SparseCore 1:
  163.6 22.1 reduce-scatter.4
  188.4 10.7 reduce-scatter.2
where the time goes:
time: 213 us; the launch traced here: 212 us
  waiting for transfers between devices  120 us (56%)
  starting transfers between devices  33.3 us (16%)
  matrix products  17.7 us (8%)
  between operations  15.6 us (7%)
  local copies, waits for them, and re-layouts  13.1 us (6%)
  other arithmetic  11.7 us (5%)
    all_to_all x1, waiting for transfers between devices, body(): lax.all_to_all(sent_rows, 'fsdp', split_axis=0, concat_axis=0, tiled=True)  107 us
    all_to_all x1, starting transfers between devices, body(): lax.all_to_all(adapter_delta.reshape(fsdp_size, capacity, value_width), '...  20.3 us
    eq x1, other arithmetic, body(): owner_index[:, None] == jnp.arange(slots_total)[None, :]  10.6 us
    all_to_all x1, waiting for transfers between devices, body(): lax.all_to_all(adapter_delta.reshape(fsdp_size, capacity, value_width), '...  9.56 us
    all_to_all x1, starting transfers between devices, body(): lax.all_to_all(sent_cot, 'fsdp', split_axis=0, concat_axis=0, tiled=True)  8.31 us
    reshape x1, local copies, waits for them, and re-layouts, body(): arrived_rows = arrived.reshape(-1, model_width)  4.76 us
    reshape x1, local copies, waits for them, and re-layouts, body(): sent_rows = sent_rows.reshape(slots_total, capacity, model_width)  4.71 us
    dot_general x1, matrix products, body(): jnp.dot(tokens, lax.all_gather(frozen_value_weight, ('fsdp', 'dp'), axis=...  4.67 us
  transfers between devices with their start and end apart: 6, of which 3 were waited for; matrix products, arithmetic and copies ran while one was open for 20% of the time, Pallas kernels for 0%

commit v1 on v0

v1 whole, which is shorter than its diff:
```python
import functools

import jax
import jax.numpy as jnp
from jax import lax
from jax.experimental import pallas as pl
from jax.experimental.pallas import tpu as pltpu
from jax.sharding import PartitionSpec as P

MESH = pl.DeviceIdType.MESH
F32 = jnp.float32
BF16 = jnp.bfloat16
PIECES = 4
GROUP = 8


def kernel(
    F, D, NZ,
    tok, de, cot, w, dn, upq, upst, s8, s8t, mask, bias,
    values, gd, gu,
    send, recv, wfull, part, re, ret, back,
    send_sem, recv_sem, wz_send, wz_recv, wp_send, wp_recv, ws_send, ws_recv,
    pt_send, pt_recv, rt_send, rt_recv,
):
    Q = PIECES
    N = F * D
    f, d = lax.axis_index("fsdp"), lax.axis_index("dp")
    me = f * D + d
    z, xy = f // 4, f % 4
    rows, C = send.shape[2], send.shape[3]
    V = cot.shape[1]
    VQ = V // Q
    CQ = C - VQ
    MD = CQ * Q
    R = dn.shape[1] // Q
    capp = rows // Q

    def remote(src, dst, ss, rs, dev):
        return pltpu.make_async_remote_copy(
            src_ref=src, dst_ref=dst, send_sem=ss, recv_sem=rs, device_id=dev, device_id_type=MESH
        )

    barrier = pltpu.get_barrier_semaphore()

    @pl.loop(0, N)
    def _(i):
        @pl.when(i != me)
        def _():
            pl.semaphore_signal(barrier, inc=1, device_id=(i // D, i % D), device_id_type=MESH)

    pl.semaphore_wait(barrier, N - 1)

    own_w = pltpu.make_async_copy(w, wfull.at[z, xy, d], wz_recv.at[0])
    own_w.start()
    z_copies = []
    for k in range(1, NZ):
        to = lax.rem(z + k, NZ)
        z_copies.append(
            remote(w, wfull.at[z, xy, d], wz_send.at[k], wz_recv.at[k], (to * 4 + xy, d))
        )
    for c in z_copies:
        c.start()

    nb = min(256, CQ)
    cot_cat = jnp.concatenate([cot[:, q * VQ:(q + 1) * VQ] for q in range(Q)], 0)
    cot_rows = jnp.dot(de[...], cot_cat, preferred_element_type=F32).astype(BF16)
    cot_rows = cot_rows.reshape(F, rows, VQ)
    for dd in range(D):
        for n in range(CQ // nb):
            piece = jnp.concatenate(
                [tok[:, dd * MD + q * CQ + n * nb:dd * MD + q * CQ + (n + 1) * nb] for q in range(Q)], 0
            )
            out = jnp.dot(de[...], piece, preferred_element_type=F32).astype(BF16)
            send[dd, :, :, n * nb:(n + 1) * nb] = out.reshape(F, rows, nb)
        send[dd, :, :, CQ:] = cot_rows

        @pl.loop(0, F)
        def _(k):
            a = lax.rem(f + k, F)
            is_me = jnp.logical_and(a == f, d == dd)

            @pl.when(is_me)
            def _():
                pltpu.make_async_copy(send.at[dd, a], recv.at[me], recv_sem).start()

            @pl.when(jnp.logical_not(is_me))
            def _():
                remote(send.at[dd, a], recv.at[me], send_sem, recv_sem, (a, dd)).start()

    own_w.wait()
    for c in z_copies:
        c.wait()
    xn, yn = xy + 1 - 2 * (xy % 2), lax.rem(xy + 2, 4)
    line = lambda p: wfull.at[:, p, d]
    p_copies = [
        remote(line(xy), line(xy), wp_send.at[0], wp_recv.at[0], (z * 4 + xn, d)),
        remote(line(xy), line(xy), wp_send.at[1], wp_recv.at[1], (z * 4 + yn, d)),
    ]
    for c in p_copies:
        c.start()
    s_copies = []

    def share(p, slot):
        for k in range(1, D):
            c = remote(
                line(p), line(p), ws_send.at[slot, k], ws_recv.at[slot, k], (f, lax.rem(d + k, D))
            )
            c.start()
            s_copies.append(c)

    share(xy, 0)
    half = NZ // 2
    top = lambda p: wfull.at[0:half, p, d]
    low_half = lambda p: wfull.at[half:NZ, p, d]
    p_copies[0].wait()
    c2 = remote(top(xn), top(xn), wp_send.at[2], wp_recv.at[2], (z * 4 + yn, d))
    c2.start()
    share(xn, 1)
    p_copies[1].wait()
    c3 = remote(low_half(yn), low_half(yn), wp_send.at[3], wp_recv.at[3], (z * 4 + xn, d))
    c3.start()
    share(yn, 2)
    c2.wait()
    c3.wait()
    share(3 - xy, 3)
    for c in s_copies:
        c.wait()

    total = jnp.broadcast_to(bias[...].astype(F32), (tok.shape[0], V))
    M = tok.shape[1]
    steps = NZ
    kk = M // steps
    for i in range(steps):
        block = wfull[i].reshape(kk, V)
        total = total + jnp.dot(tok[:, i * kk:(i + 1) * kk], block, preferred_element_type=F32)

    pltpu.make_async_copy(recv, recv, recv_sem).wait()
    G = GROUP
    gr, gc = G * rows, G * capp

    def gather_rows(x):
        x = x * mask[...]
        hi = x.astype(BF16)
        r1 = x - hi.astype(F32)
        mid = r1.astype(BF16)
        lo = (r1 - mid.astype(F32)).astype(BF16)
        y = jnp.dot(s8[...], hi, preferred_element_type=F32)
        y = y + jnp.dot(s8[...], mid, preferred_element_type=F32)
        y = y + jnp.dot(s8[...], lo, preferred_element_type=F32)
        return sum([y[:, q * R:(q + 1) * R] for q in range(Q)])

    def spread_rows(x):
        x = jnp.concatenate([x] * Q, 1)
        return (jnp.dot(s8t[...], x, preferred_element_type=F32) * mask[...]).astype(BF16)

    @pl.loop(0, N // G)
    def _(g):
        x = recv[pl.ds(g * G, G), :, 0:CQ].reshape(gr, CQ)
        p = gather_rows(jnp.dot(x, dn[...], preferred_element_type=F32))
        part[d, pl.ds(pl.multiple_of(g * gc, 8), gc), :] = jnp.concatenate([p] * (128 // R), 1)
        c = recv[pl.ds(g * G, G), :, CQ:C].reshape(gr, VQ)
        rc = gather_rows(jnp.dot(c, upq[...], preferred_element_type=F32)).astype(BF16)
        re[g] = spread_rows(rc)

    pt_copies = [
        remote(part.at[d], part.at[d], pt_send.at[k], pt_recv.at[k], (f, lax.rem(d + k, D)))
        for k in range(1, D)
    ]
    for c in pt_copies:
        c.start()
    for c in pt_copies:
        c.wait()
    gu[...] = jnp.zeros_like(gu)

    @pl.loop(0, N // G)
    def _(g):
        at = pl.ds(pl.multiple_of(g * gc, 8), gc)
        low = sum([part[k, at, 0:R] for k in range(D)]).astype(BF16)
        le = spread_rows(low)
        ret[pl.ds(g * G, G)] = (
            jnp.dot(le, upst[...], preferred_element_type=F32).astype(BF16).reshape(G, rows, VQ)
        )
        c = recv[pl.ds(g * G, G), :, CQ:C].reshape(gr, VQ)
        gu[...] += lax.dot_general(le, c, (((0,), (0,)), ((), ())), preferred_element_type=F32)

    @pl.loop(0, F)
    def _(k):
        s = lax.rem(f + k, F)

        @pl.when(s == f)
        def _():
            pltpu.make_async_copy(ret.at[s * D + d], back.at[f], rt_recv).start()

        @pl.when(s != f)
        def _():
            remote(ret.at[s * D + d], back.at[f], rt_send, rt_recv, (s, d)).start()

    gd[...] = jnp.zeros_like(gd)

    @pl.loop(0, N // G)
    def _(g):
        x = recv[pl.ds(g * G, G), :, 0:CQ].reshape(gr, CQ)
        gd[...] += lax.dot_general(x, re[g], (((0,), (0,)), ((), ())), preferred_element_type=F32)

    pltpu.make_async_copy(back, back, rt_recv).wait()
    T = tok.shape[0]
    b = back[...].reshape(F * rows, VQ)
    placed = lax.dot_general(de[...], b, (((0,), (0,)), ((), ())), preferred_element_type=F32)
    placed = jnp.concatenate([placed[q * T:(q + 1) * T] for q in range(Q)], 1)
    values[...] = (total + placed).astype(BF16)

    pltpu.make_async_copy(recv.at[0:N - 1], recv.at[0:N - 1], send_sem).wait()
    pltpu.make_async_copy(back.at[0:F - 1], back.at[0:F - 1], rt_send).wait()


def body(tokens, token_adapter_index, adapter_storage_index, weight, bias, down, up, cotangent):
    F, D = lax.axis_size("fsdp"), lax.axis_size("dp")
    T, M = tokens.shape
    V = weight.shape[1]
    A = adapter_storage_index.shape[0]
    R = down.shape[2]
    Q = PIECES
    N = F * D
    cap = max(2, (3 * T + 2 * F - 1) // (2 * F))
    capp = -(-cap // Q) * Q
    rows = Q * capp
    MD, VQ = M // D, V // Q
    CQ = MD // Q
    NZ = F // 4
    d = lax.axis_index("dp")

    hot = token_adapter_index == jnp.arange(A)[None, :]
    owner = jnp.sum(jnp.where(hot, adapter_storage_index[None, :], 0), 1)
    i = jnp.arange(T)
    same = (owner[:, None] == owner[None, :]) & (i[None, :] < i[:, None])
    target = owner * capp + jnp.sum(same.astype(jnp.int32), 1)
    code = jnp.arange(A)[:, None, None] * capp + jnp.arange(capp)[None, None, :]
    code = jnp.broadcast_to(code, (A, Q, capp)).reshape(A * rows, 1, 1)
    q_row = jnp.broadcast_to(jnp.arange(Q)[None, :, None], (A, Q, capp)).reshape(A * rows, 1, 1)
    de = (code == target[None, None, :]) & (q_row == jnp.arange(Q)[None, :, None])
    de = de.astype(BF16).reshape(A * rows, Q * T)

    mine = lax.dynamic_slice_in_dim(down[0], d * MD, MD, 0)
    dn = mine.reshape(Q, CQ, R).transpose(1, 0, 2).reshape(CQ, Q * R)
    upst = up[0].reshape(R, Q, VQ).transpose(1, 0, 2).reshape(Q * R, VQ)
    upq = upst.T

    gr, gc = GROUP * rows, GROUP * capp
    rr, cc = jnp.arange(gr), jnp.arange(gc)
    from_row = (rr // rows) * capp + rr % capp
    s8t = (from_row[:, None] == cc[None, :]).astype(BF16)
    s8 = s8t.T
    mask = (((rr % rows) // capp)[:, None] == (jnp.arange(Q * R) // R)[None, :]).astype(F32)

    vmem = pl.BlockSpec(memory_space=pltpu.VMEM)
    dma = pltpu.SemaphoreType.DMA
    values, gd, gu = pl.pallas_call(
        functools.partial(kernel, F, D, NZ),
        out_shape=(
            jax.ShapeDtypeStruct((T, V), BF16),
            jax.ShapeDtypeStruct((CQ, Q * R), F32),
            jax.ShapeDtypeStruct((Q * R, VQ), F32),
        ),
        in_specs=[vmem] * 11,
        out_specs=(vmem,) * 3,
        scratch_shapes=[
            pltpu.VMEM((D, F, rows, CQ + VQ), BF16),
            pltpu.VMEM((N, rows, CQ + VQ), BF16),
            pltpu.VMEM((NZ, 4, D, M // N, V), BF16),
            pltpu.VMEM((D, N * capp, 128), F32),
            pltpu.VMEM((N // GROUP, gr, Q * R), BF16),
            pltpu.VMEM((N, rows, VQ), BF16),
            pltpu.VMEM((F, rows, VQ), BF16),
            dma, dma,
            dma((NZ,)), dma((NZ,)),
            dma((4,)), dma((4,)),
            dma((4, D)), dma((4, D)),
            dma((D,)), dma((D,)),
            dma, dma,
        ],
        compiler_params=pltpu.CompilerParams(
            collective_id=0, has_side_effects=True, vmem_limit_bytes=56 * 2**20
        ),
    )(tokens, de, cotangent, weight, dn, upq, upst, s8, s8t, mask, bias[None, :])
    gd = gd.reshape(CQ, Q, R).transpose(1, 0, 2).reshape(1, MD, R)
    gu = gu.reshape(Q, R, VQ).transpose(1, 0, 2).reshape(R, V)
    gu = lax.dynamic_slice_in_dim(gu, d * (V // D), V // D, 1)[None]
    return values, gd, gu


def solution(mesh):
    return jax.shard_map(
        body,
        mesh=mesh,
        in_specs=(
            P(("fsdp", "dp"), None),
            P(("fsdp", "dp"), None),
            P(),
            P(("fsdp", "dp"), None),
            P(),
            P("fsdp", None, None),
            P("fsdp", None, None),
            P(("fsdp", "dp"), None),
        ),
        out_specs=(P(("fsdp", "dp"), None), P("fsdp", "dp", None), P("fsdp", None, "dp")),
        check_vma=False,
    )
```

time: 213 us -> 151 us (0.71)
  Pallas kernels: 0 us -> 131 us
  waiting for transfers between devices: 120 us -> 0 us
  starting transfers between devices: 33.3 us -> 0 us
  matrix products: 17.7 us -> 0 us
  between operations: 15.6 us -> 0.8 us
  other arithmetic: 11.7 us -> 7.09 us
    pallas_call x0 -> x1, Pallas kernels: none -> 131 us  [body(): pl.pallas_call(functools.partial(kernel, F, D, NZ), out_shape=(jax.ShapeD...]
    all_to_all x3 -> x0, waiting for transfers between devices: 120 us -> none  [the longest x1 107 us: body(): lax.all_to_all(sent_rows, 'fsdp', split_axis=0, concat_axis=0, tiled=True)]
    all_to_all x3 -> x0, starting transfers between devices: 33.2 us -> none  [the longest x1 20.3 us: body(): lax.all_to_all(adapter_delta.reshape(fsdp_size, capacity, value_width), '...]
    dot_general x8 -> x0, matrix products: 17.7 us -> none  [the longest x1 4.67 us: body(): jnp.dot(tokens, lax.all_gather(frozen_value_weight, ('fsdp', 'dp'), axis=...]
    eq x1 -> x2, other arithmetic: 10.6 us -> 0.34 us  [the longest x1 0.17 us: body(): q_row == jnp.arange(Q)[None, :, None]]
    reshape x6 -> x4, local copies, waits for them, and re-layouts: 11.1 us -> 4.08 us  [the longest x1 1.69 us: body(): gd = gd.reshape(CQ, Q, R).transpose(1, 0, 2).reshape(1, MD, R)]
    convert_element_type x2 -> x4, other arithmetic: 0.09 us -> 5.62 us  [the longest x1 3.37 us: body(): de = de.astype(BF16).reshape(A * rows, Q * T)]
  transfers between devices with their start and end apart: 6 -> 0, of which waited for: 3 -> 0; matrix products, arithmetic and copies ran while one was open for 20% -> 0% of each run, Pallas kernels for 0% -> 0%
where the time goes in v1:
time: 151 us
  Pallas kernels  131 us (87%)
  local copies, waits for them, and re-layouts  12 us (8%)
  other arithmetic  7.09 us (5%)
    pallas_call x1, Pallas kernels, body(): pl.pallas_call(functools.partial(kernel, F, D, NZ), out_shape=(jax.ShapeD...  131 us
    convert_element_type x1, other arithmetic, body(): de = de.astype(BF16).reshape(A * rows, Q * T)  3.37 us

profile of v1, /device:TPU:0, one launch (start us, length us, event | category | flops | bytes accessed | tf_op | source)
XLA Modules:
  0.0 150.9 jit_solution(13115367524370518350)
XLA Ops:
  0.7 0.8 select_reduce_fusion
  1.5 0.2 convert_reduce_fusion
  1.7 1.3 broadcast_in_dim.24.bias
  3.1 0.1 eq.104
  3.2 0.1 eq.115
  3.3 0.9 reshape_squeeze.3
  4.2 0.7 copy.30.upq
  5.0 0.6 fusion.1.s8
  5.6 0.2 broadcast_compare_fusion
  5.8 0.2 iota_compare_fusion
  6.0 0.8 fusion.s8t
  6.7 0.9 compare_convert_fusion.mask
  7.6 0.4 reshape.179
  8.0 0.2 copy.27
  8.2 1.0 copy.29.dn
  9.2 3.4 %and_convert_fusion = bf16[768,4,128]{2,1,0:T(4,128)(2,1)S(1)} fusion(pred[768,4]{1,0:T(8,128)(4,1)S(1)} %iota_compare_fusion, pred[768,128]{1,0:T(8,128)(4,1)S(1)} %broadcast_compare_fusion), kind=kLoop, calls=%fused_computation | loop fusion | flops 786432 | bytes 887808 | tf_op jit(solution)/shard_map/convert_element_type | solution.py:241
  12.6 1.0 copy.38
  13.6 131.1 %shard_map.103 = (bf16[128,512]{1,0:T(8,128)(2,1)}, f32[1024,256]{1,0:T(8,128)}, f32[256,128]{1,0:T(8,128)}) custom-call(bf16[128,8192]{1,0:T(8,128)(2,1)} %tok.1, bf16[768,512]{1,0:T(8,128)(2,1)} %bitcast.29, bf16[128,512]{1,0:T(8,128)(2,1)} %cot.1, bf16[256,512]{1,0:T(8,128)(2,1)} %w.1, bf16[1024,256]{1,0:T(8,128)(2,1)} %copy.29.dn, ...), custom_call_target="tpu_custom_call" | custom-call | tf_op jit(solution)/shard_map/pallas_call | solution.py:257
  144.7 1.0 copy.33
  145.7 0.6 dynamic-slice_bitcast_fusion
  146.3 1.6 %copy.31 = f32[1024,256]{0,1:T(8,128)S(1)} copy(f32[1024,256]{1,0:T(8,128)} %get-tuple-element.7) | data formatting | bytes 2097152 | tf_op jit(solution)/shard_map/pallas_call | solution.py:257
  147.9 0.7 copy.32
  148.6 1.7 %reshape.183 = f32[1,4096,64]{1,2,0:T(8,128)} reshape(f32[4,1024,64]{1,0,2:T(4,128)S(1)} %copy.32) | data formatting | bytes 2097152 | tf_op jit(solution)/shard_map/reshape | solution.py:285
  150.3 0.7 copy.41
  (17 shorter events, 0.2 us)
Async XLA Ops:
  0.6 6.9 %copy-start = (bf16[1,8192,64]{1,2,0:T(8,128)(2,1)S(1)}, bf16[1,8192,64]{1,2,0:T(8,128)(2,1)}, u32[]{:S(2)}) copy-start(bf16[1,8192,64]{1,2,0:T(8,128)(2,1)} %param.13) | copy-start | bytes 3145732
  4.2 5.0 %copy-start.1 = (bf16[64,4,128]{2,0,1:T(8,128)(2,1)}, bf16[64,4,128]{2,0,1:T(8,128)(2,1)S(1)}, u32[]{:S(2)}) copy-start(bf16[64,4,128]{2,0,1:T(8,128)(2,1)S(1)} %copy.28) | copy-start | bytes 196612
  147.9 2.4 %copy-start.2 = (bf16[128,512]{1,0:T(8,128)(2,1)S(1)}, bf16[128,512]{1,0:T(8,128)(2,1)}, u32[]{:S(2)}) copy-start(bf16[128,512]{1,0:T(8,128)(2,1)} %get-tuple-element.12) | copy-start | bytes 393220

commit v2 on v1

--- a/solution.py
+++ b/solution.py
@@ -2,6 +2,7 @@
 
 import jax
 import jax.numpy as jnp
+import numpy as np
 from jax import lax
 from jax.experimental import pallas as pl
 from jax.experimental.pallas import tpu as pltpu
@@ -120,19 +121,6 @@
     c3 = remote(low_half(yn), low_half(yn), wp_send.at[3], wp_recv.at[3], (z * 4 + xn, d))
     c3.start()
     share(yn, 2)
-    c2.wait()
-    c3.wait()
-    share(3 - xy, 3)
-    for c in s_copies:
-        c.wait()
-
-    total = jnp.broadcast_to(bias[...].astype(F32), (tok.shape[0], V))
-    M = tok.shape[1]
-    steps = NZ
-    kk = M // steps
-    for i in range(steps):
-        block = wfull[i].reshape(kk, V)
-        total = total + jnp.dot(tok[:, i * kk:(i + 1) * kk], block, preferred_element_type=F32)
 
     pltpu.make_async_copy(recv, recv, recv_sem).wait()
     G = GROUP
@@ -195,12 +183,27 @@
         def _():
             remote(ret.at[s * D + d], back.at[f], rt_send, rt_recv, (s, d)).start()
 
+    c2.wait()
+    c3.wait()
+    share(3 - xy, 3)
+
     gd[...] = jnp.zeros_like(gd)
 
     @pl.loop(0, N // G)
     def _(g):
         x = recv[pl.ds(g * G, G), :, 0:CQ].reshape(gr, CQ)
         gd[...] += lax.dot_general(x, re[g], (((0,), (0,)), ((), ())), preferred_element_type=F32)
+
+    for c in s_copies:
+        c.wait()
+
+    total = jnp.broadcast_to(bias[...].astype(F32), (tok.shape[0], V))
+    M = tok.shape[1]
+    steps = NZ
+    kk = M // steps
+    for i in range(steps):
+        block = wfull[i].reshape(kk, V)
+        total = total + jnp.dot(tok[:, i * kk:(i + 1) * kk], block, preferred_element_type=F32)
 
     pltpu.make_async_copy(back, back, rt_recv).wait()
     T = tok.shape[0]
@@ -246,11 +249,11 @@
     upq = upst.T
 
     gr, gc = GROUP * rows, GROUP * capp
-    rr, cc = jnp.arange(gr), jnp.arange(gc)
+    rr, cc = np.arange(gr), np.arange(gc)
     from_row = (rr // rows) * capp + rr % capp
     s8t = (from_row[:, None] == cc[None, :]).astype(BF16)
     s8 = s8t.T
-    mask = (((rr % rows) // capp)[:, None] == (jnp.arange(Q * R) // R)[None, :]).astype(F32)
+    mask = (((rr % rows) // capp)[:, None] == (np.arange(Q * R) // R)[None, :]).astype(np.float32)
 
     vmem = pl.BlockSpec(memory_space=pltpu.VMEM)
     dma = pltpu.SemaphoreType.DMA

time: 151 us -> 147 us (0.974)
  other arithmetic: 7.09 us -> 4.81 us
    convert_element_type x3 -> x0, other arithmetic: 2.25 us -> none  [the longest x2 1.4 us: body(): s8t = (from_row[:, None] == cc[None, :]).astype(BF16)]
where the time goes in v2:
time: 147 us
  Pallas kernels  130 us (88%)
  local copies, waits for them, and re-layouts  12 us (8%)
  other arithmetic  4.81 us (3%)
    pallas_call x1, Pallas kernels, body(): pl.pallas_call(functools.partial(kernel, F, D, NZ), out_shape=(jax.ShapeD...  130 us
    convert_element_type x1, other arithmetic, body(): de = de.astype(BF16).reshape(A * rows, Q * T)  3.37 us

profile of v2, /device:TPU:0, one launch (start us, length us, event | category | flops | bytes accessed | tf_op | source)
XLA Modules:
  0.0 147.2 jit_solution(9040402895253631283)
XLA Ops:
  0.6 0.0 copy-start
  0.7 0.8 select_reduce_fusion
  1.5 0.2 convert_reduce_fusion
  1.7 1.3 broadcast_in_dim.24.bias
  3.0 0.1 iota_add_fusion
  3.1 0.1 eq.68
  3.2 0.1 eq.79
  3.3 0.9 reshape_squeeze.3
  4.2 0.0 copy-start.1
  4.2 0.7 copy.33.upq
  4.9 0.2 broadcast_compare_fusion
  5.1 0.2 iota_compare_fusion
  5.3 0.4 reshape.130
  5.7 0.2 copy.30
  5.9 1.0 copy.32.dn
  6.9 3.4 %and_convert_fusion = bf16[768,4,128]{2,1,0:T(4,128)(2,1)S(1)} fusion(pred[768,4]{1,0:T(8,128)(4,1)S(1)} %iota_compare_fusion, pred[768,128]{1,0:T(8,128)(4,1)S(1)} %broadcast_compare_fusion), kind=kLoop, calls=%fused_computation | loop fusion | flops 786432 | bytes 887808 | tf_op jit(solution)/shard_map/convert_element_type | solution.py:244
  10.3 1.0 copy.41
  11.3 129.7 %shard_map.130 = (bf16[128,512]{1,0:T(8,128)(2,1)}, f32[1024,256]{1,0:T(8,128)}, f32[256,128]{1,0:T(8,128)}) custom-call(bf16[128,8192]{1,0:T(8,128)(2,1)} %tok.1, bf16[768,512]{1,0:T(8,128)(2,1)} %bitcast.29, bf16[128,512]{1,0:T(8,128)(2,1)} %cot.1, bf16[256,512]{1,0:T(8,128)(2,1)} %w.1, bf16[1024,256]{1,0:T(8,128)(2,1)} %copy.32.dn, ...), custom_call_target="tpu_custom_call" | custom-call | tf_op jit(solution)/shard_map/pallas_call | solution.py:260
  141.0 1.0 copy.36
  142.0 0.6 dynamic-slice_bitcast_fusion
  142.6 1.6 %copy.34 = f32[1024,256]{0,1:T(8,128)S(1)} copy(f32[1024,256]{1,0:T(8,128)} %get-tuple-element.7) | data formatting | bytes 2097152 | tf_op jit(solution)/shard_map/pallas_call | solution.py:260
  144.2 0.7 copy.35
  144.9 1.7 %reshape.134 = f32[1,4096,64]{1,2,0:T(8,128)} reshape(f32[4,1024,64]{1,0,2:T(4,128)S(1)} %copy.35) | data formatting | bytes 2097152 | tf_op jit(solution)/shard_map/reshape | solution.py:288
  146.6 0.7 copy.44
  (11 shorter events, 0.1 us)
Async XLA Ops:
  0.6 4.7 %copy-start = (bf16[1,8192,64]{1,2,0:T(8,128)(2,1)S(1)}, bf16[1,8192,64]{1,2,0:T(8,128)(2,1)}, u32[]{:S(2)}) copy-start(bf16[1,8192,64]{1,2,0:T(8,128)(2,1)} %param.16) | copy-start | bytes 3145732
  4.2 2.7 %copy-start.1 = (bf16[64,4,128]{2,0,1:T(8,128)(2,1)}, bf16[64,4,128]{2,0,1:T(8,128)(2,1)S(1)}, u32[]{:S(2)}) copy-start(bf16[64,4,128]{2,0,1:T(8,128)(2,1)S(1)} %copy.31) | copy-start | bytes 196612
  144.2 2.4 %copy-start.2 = (bf16[128,512]{1,0:T(8,128)(2,1)S(1)}, bf16[128,512]{1,0:T(8,128)(2,1)}, u32[]{:S(2)}) copy-start(bf16[128,512]{1,0:T(8,128)(2,1)} %get-tuple-element.12) | copy-start | bytes 393220

commit v3 on v2

--- a/solution.py
+++ b/solution.py
@@ -77,7 +77,7 @@
 
         @pl.loop(0, F)
         def _(k):
-            a = lax.rem(f + k, F)
+            a = lax.rem(f + F // 2 + k, F)
             is_me = jnp.logical_and(a == f, d == dd)
 
             @pl.when(is_me)

time: 147 us -> 144 us (0.980)
  Pallas kernels: 130 us -> 126 us
    pallas_call x1, Pallas kernels: 130 us -> 126 us  [body(): pl.pallas_call(functools.partial(kernel, F, D, NZ), out_shape=(jax.ShapeD...]
where the time goes in v3:
time: 144 us
  Pallas kernels  126 us (88%)
  local copies, waits for them, and re-layouts  12 us (8%)
  other arithmetic  4.81 us (3%)
    pallas_call x1, Pallas kernels, body(): pl.pallas_call(functools.partial(kernel, F, D, NZ), out_shape=(jax.ShapeD...  126 us
    convert_element_type x1, other arithmetic, body(): de = de.astype(BF16).reshape(A * rows, Q * T)  3.37 us

profile of v3, /device:TPU:0, one launch (start us, length us, event | category | flops | bytes accessed | tf_op | source)
XLA Modules:
  0.0 143.7 jit_solution(702267519341973432)
XLA Ops:
  0.6 0.0 copy-start
  0.7 0.8 select_reduce_fusion
  1.5 0.2 convert_reduce_fusion
  1.7 1.3 broadcast_in_dim.24.bias
  3.0 0.1 iota_add_fusion
  3.1 0.1 eq.68
  3.2 0.1 eq.79
  3.3 0.9 reshape_squeeze.3
  4.2 0.0 copy-start.1
  4.2 0.7 copy.33.upq
  4.9 0.2 broadcast_compare_fusion
  5.1 0.2 iota_compare_fusion
  5.3 0.4 reshape.130
  5.7 0.2 copy.30
  5.9 1.0 copy.32.dn
  6.9 3.4 %and_convert_fusion = bf16[768,4,128]{2,1,0:T(4,128)(2,1)S(1)} fusion(pred[768,4]{1,0:T(8,128)(4,1)S(1)} %iota_compare_fusion, pred[768,128]{1,0:T(8,128)(4,1)S(1)} %broadcast_compare_fusion), kind=kLoop, calls=%fused_computation | loop fusion | flops 786432 | bytes 887808 | tf_op jit(solution)/shard_map/convert_element_type | solution.py:244
  10.3 1.0 copy.41
  11.3 126.1 %shard_map.130 = (bf16[128,512]{1,0:T(8,128)(2,1)}, f32[1024,256]{1,0:T(8,128)}, f32[256,128]{1,0:T(8,128)}) custom-call(bf16[128,8192]{1,0:T(8,128)(2,1)} %tok.1, bf16[768,512]{1,0:T(8,128)(2,1)} %bitcast.29, bf16[128,512]{1,0:T(8,128)(2,1)} %cot.1, bf16[256,512]{1,0:T(8,128)(2,1)} %w.1, bf16[1024,256]{1,0:T(8,128)(2,1)} %copy.32.dn, ...), custom_call_target="tpu_custom_call" | custom-call | tf_op jit(solution)/shard_map/pallas_call | solution.py:260
  137.4 1.0 copy.36
  138.4 0.6 dynamic-slice_bitcast_fusion
  139.1 1.6 %copy.34 = f32[1024,256]{0,1:T(8,128)S(1)} copy(f32[1024,256]{1,0:T(8,128)} %get-tuple-element.7) | data formatting | bytes 2097152 | tf_op jit(solution)/shard_map/pallas_call | solution.py:260
  140.6 0.7 copy.35
  141.3 1.7 %reshape.134 = f32[1,4096,64]{1,2,0:T(8,128)} reshape(f32[4,1024,64]{1,0,2:T(4,128)S(1)} %copy.35) | data formatting | bytes 2097152 | tf_op jit(solution)/shard_map/reshape | solution.py:288
  143.0 0.7 copy.44
  (11 shorter events, 0.1 us)
Async XLA Ops:
  0.6 4.7 %copy-start = (bf16[1,8192,64]{1,2,0:T(8,128)(2,1)S(1)}, bf16[1,8192,64]{1,2,0:T(8,128)(2,1)}, u32[]{:S(2)}) copy-start(bf16[1,8192,64]{1,2,0:T(8,128)(2,1)} %param.16) | copy-start | bytes 3145732
  4.2 2.7 %copy-start.1 = (bf16[64,4,128]{2,0,1:T(8,128)(2,1)}, bf16[64,4,128]{2,0,1:T(8,128)(2,1)S(1)}, u32[]{:S(2)}) copy-start(bf16[64,4,128]{2,0,1:T(8,128)(2,1)S(1)} %copy.31) | copy-start | bytes 196612
  140.6 2.4 %copy-start.2 = (bf16[128,512]{1,0:T(8,128)(2,1)S(1)}, bf16[128,512]{1,0:T(8,128)(2,1)}, u32[]{:S(2)}) copy-start(bf16[128,512]{1,0:T(8,128)(2,1)} %get-tuple-element.12) | copy-start | bytes 393220

commit v4 on v3

--- a/solution.py
+++ b/solution.py
@@ -75,9 +75,16 @@
             send[dd, :, :, n * nb:(n + 1) * nb] = out.reshape(F, rows, nb)
         send[dd, :, :, CQ:] = cot_rows
 
-        @pl.loop(0, F)
+        @pl.loop(0, F // 2)
         def _(k):
-            a = lax.rem(f + F // 2 + k, F)
+            a = (1 - f // (F // 2)) * (F // 2) + lax.rem(f + k, F // 2)
+            remote(send.at[dd, a], recv.at[me], send_sem, recv_sem, (a, dd)).start()
+
+    for dd in range(D):
+
+        @pl.loop(0, F // 2)
+        def _(k):
+            a = (f // (F // 2)) * (F // 2) + lax.rem(f + k, F // 2)
             is_me = jnp.logical_and(a == f, d == dd)
 
             @pl.when(is_me)

time: 144 us -> 148 us (1.028)
  Pallas kernels: 126 us -> 129 us
    pallas_call x1, Pallas kernels: 126 us -> 129 us  [body(): pl.pallas_call(functools.partial(kernel, F, D, NZ), out_shape=(jax.ShapeD...]
where the time goes in v4:
time: 148 us; the launch traced here: 147 us
  Pallas kernels  129 us (87%)
  local copies, waits for them, and re-layouts  12 us (8%)
  other arithmetic  4.81 us (3%)
    pallas_call x1, Pallas kernels, body(): pl.pallas_call(functools.partial(kernel, F, D, NZ), out_shape=(jax.ShapeD...  129 us
    convert_element_type x1, other arithmetic, body(): de = de.astype(BF16).reshape(A * rows, Q * T)  3.37 us

profile of v4, /device:TPU:0, one launch (start us, length us, event | category | flops | bytes accessed | tf_op | source)
XLA Modules:
  0.0 146.9 jit_solution(13494899000136855713)
XLA Ops:
  0.6 0.0 copy-start
  0.7 0.8 select_reduce_fusion
  1.5 0.2 convert_reduce_fusion
  1.7 1.3 broadcast_in_dim.24.bias
  3.0 0.1 iota_add_fusion
  3.1 0.1 eq.68
  3.2 0.1 eq.79
  3.3 0.9 reshape_squeeze.3
  4.2 0.0 copy-start.1
  4.2 0.7 copy.33.upq
  4.9 0.2 broadcast_compare_fusion
  5.1 0.2 iota_compare_fusion
  5.3 0.4 reshape.130
  5.7 0.2 copy.30
  5.9 1.0 copy.32.dn
  6.9 3.4 %and_convert_fusion = bf16[768,4,128]{2,1,0:T(4,128)(2,1)S(1)} fusion(pred[768,4]{1,0:T(8,128)(4,1)S(1)} %iota_compare_fusion, pred[768,128]{1,0:T(8,128)(4,1)S(1)} %broadcast_compare_fusion), kind=kLoop, calls=%fused_computation | loop fusion | flops 786432 | bytes 887808 | tf_op jit(solution)/shard_map/convert_element_type | solution.py:251
  10.3 1.0 copy.41
  11.3 129.3 %shard_map.130 = (bf16[128,512]{1,0:T(8,128)(2,1)}, f32[1024,256]{1,0:T(8,128)}, f32[256,128]{1,0:T(8,128)}) custom-call(bf16[128,8192]{1,0:T(8,128)(2,1)} %tok.1, bf16[768,512]{1,0:T(8,128)(2,1)} %bitcast.29, bf16[128,512]{1,0:T(8,128)(2,1)} %cot.1, bf16[256,512]{1,0:T(8,128)(2,1)} %w.1, bf16[1024,256]{1,0:T(8,128)(2,1)} %copy.32.dn, ...), custom_call_target="tpu_custom_call" | custom-call | tf_op jit(solution)/shard_map/pallas_call | solution.py:267
  140.6 1.0 copy.36
  141.6 0.6 dynamic-slice_bitcast_fusion
  142.3 1.6 %copy.34 = f32[1024,256]{0,1:T(8,128)S(1)} copy(f32[1024,256]{1,0:T(8,128)} %get-tuple-element.7) | data formatting | bytes 2097152 | tf_op jit(solution)/shard_map/pallas_call | solution.py:267
  143.9 0.7 copy.35
  144.5 1.7 %reshape.134 = f32[1,4096,64]{1,2,0:T(8,128)} reshape(f32[4,1024,64]{1,0,2:T(4,128)S(1)} %copy.35) | data formatting | bytes 2097152 | tf_op jit(solution)/shard_map/reshape | solution.py:295
  146.2 0.7 copy.44
  (11 shorter events, 0.1 us)
Async XLA Ops:
  0.6 4.7 %copy-start = (bf16[1,8192,64]{1,2,0:T(8,128)(2,1)S(1)}, bf16[1,8192,64]{1,2,0:T(8,128)(2,1)}, u32[]{:S(2)}) copy-start(bf16[1,8192,64]{1,2,0:T(8,128)(2,1)} %param.16) | copy-start | bytes 3145732
  4.2 2.7 %copy-start.1 = (bf16[64,4,128]{2,0,1:T(8,128)(2,1)}, bf16[64,4,128]{2,0,1:T(8,128)(2,1)S(1)}, u32[]{:S(2)}) copy-start(bf16[64,4,128]{2,0,1:T(8,128)(2,1)S(1)} %copy.31) | copy-start | bytes 196612
  143.8 2.4 %copy-start.2 = (bf16[128,512]{1,0:T(8,128)(2,1)S(1)}, bf16[128,512]{1,0:T(8,128)(2,1)}, u32[]{:S(2)}) copy-start(bf16[128,512]{1,0:T(8,128)(2,1)} %get-tuple-element.12) | copy-start | bytes 393220
